TPU v7x, 32 devices: a whole 2x2x4 slice. The times are simulated.
32 devices in a mesh: blk: 2 (over x), wide: 4 (over z), rep: 4 (over y, core).
Axes of the slice: x: 2, y: 2, z: 4, core: 2. Of those that a mesh axis runs over, the one named last changes fastest.
Arguments:
- amplitudes: bfloat16 [8192, 4096], P(('rep', 'wide'), 'blk'), may hold values from -6 to 6
- integrals: bfloat16 [8192, 256], P('rep', 'blk'), may hold values from -0.26367188 to 0.26367188
- occ_energy: float32 [400], replicated, may hold values from -1 to -0.2
- virt_energy: float32 [1600], replicated, may hold values from 0.1 to 1
- virt_irrep: int32 [1600], replicated, may hold values from 0 to 3
- ij_pairs: int32 [4096, 2], P(('blk', 'wide')), may hold values from 0 to 399
- ab_pairs: int32 [256, 2], replicated, may hold values from 0 to 1599
- cd_pairs: int32 [8192, 2], P('rep'), may hold values from 0 to 1599
Outputs:
- new_amplitudes: bfloat16 [256, 4096], P(('rep', 'wide'), 'blk')
All inputs are finite; a program needn't handle non-finite values.
Results may differ from a plain program's by a relative error of at most 0.012.
Values may be sent and summed in bfloat16 or wider, within the bound.
A program may use at most 64 MiB of HBM per device.

v0:
```python
import jax
import jax.numpy as jnp
from jax import lax
from jax.sharding import PartitionSpec as P


def passed_along(block, axis, distance):
    devices = range(lax.axis_size(axis))
    route = [((i - distance) % len(devices), i) for i in devices]
    return lax.ppermute(block, axis, route)


def lookup(indices, source_table):
    matched = indices[:, None] == lax.broadcasted_iota(jnp.int32, (1, source_table.shape[0]), 1)
    return jnp.sum(
        jnp.where(matched, source_table[None, :], jnp.zeros_like(source_table)[None, :]), axis=1
    )


def per_device(
    amplitudes, integrals, occ_energy, virt_energy, virt_irrep, ij_pairs, ab_pairs, cd_pairs
):
    amp_rows = lax.all_to_all(amplitudes, "wide", split_axis=1, concat_axis=0, tiled=True)
    ab_labels = jnp.bitwise_xor(
        lookup(ab_pairs[:, 0], virt_irrep), lookup(ab_pairs[:, 1], virt_irrep)
    )
    cd_labels = jnp.bitwise_xor(
        lookup(cd_pairs[:, 0], virt_irrep), lookup(cd_pairs[:, 1], virt_irrep)
    )
    tile_cols = integrals.shape[1]
    cycle_size = lax.axis_size("blk")
    my_block = lax.axis_index("blk")
    partial_value = jnp.zeros((amp_rows.shape[1], tile_cols * cycle_size), jnp.float32)
    slab_tile = integrals
    for rounds in range(cycle_size):
        source = (my_block - rounds) % cycle_size
        offset = source * tile_cols
        col_labels = lax.dynamic_slice_in_dim(ab_labels, offset, slab_tile.shape[1])
        masked = jnp.where(
            cd_labels[:, None] == col_labels[None, :], slab_tile, jnp.zeros_like(slab_tile)
        )
        partial_value = lax.dynamic_update_slice_in_dim(
            partial_value,
            lax.dot_general(
                amp_rows, masked, (((0,), (0,)), ((), ())), preferred_element_type=jnp.float32
            ),
            offset,
            1,
        )
        if rounds + 1 < cycle_size:
            slab_tile = passed_along(slab_tile, "blk", 1)
    summed = lax.psum_scatter(
        partial_value.astype(jnp.bfloat16), "rep", scatter_dimension=1, tiled=True
    ).astype(jnp.float32)
    quarter = summed.shape[1]
    col_first = lax.axis_index("rep") * quarter
    ab_local = lax.dynamic_slice_in_dim(ab_pairs, col_first, quarter, 0)
    pair_virt = lookup(ab_local[:, 0], virt_energy) + lookup(ab_local[:, 1], virt_energy)
    pair_occ = lookup(ij_pairs[:, 0], occ_energy) + lookup(ij_pairs[:, 1], occ_energy)
    updated = (summed / (pair_occ[:, None] - pair_virt[None, :])).astype(jnp.bfloat16)
    return lax.all_to_all(updated.T, "wide", split_axis=0, concat_axis=1, tiled=True)


def solution(mesh):
    in_specs = (
        P(("rep", "wide"), "blk"),
        P("rep", "blk"),
        P(),
        P(),
        P(),
        P(("blk", "wide"), None),
        P(),
        P("rep", None),
    )
    out_specs = P(("rep", "wide"), "blk")
    return jax.shard_map(
        per_device, mesh=mesh, in_specs=in_specs, out_specs=out_specs, check_vma=False
    )
```

profile of v0, /device:TPU:0, one launch (start us, length us, event | category | flops | bytes accessed | tf_op | source)
XLA Modules:
  0.0 109.9 jit_solution(14807200694654213374)
XLA Ops:
  6.5 3.9 %copy.12 = bf16[512,2048]{0,1:T(8,128)(2,1)} copy(bf16[512,2048]{1,0:T(8,128)(2,1)} %param.8) | data formatting | bytes 4194304 | tf_op args[0]
  10.5 0.0 copy-start.2
  10.5 0.0 copy-start.6
  10.5 0.0 copy-start.5
  10.5 0.0 copy-start.3
  10.5 6.5 %all-to-all-start = ((bf16[512,4,512]{0,2,1:T(8,128)(2,1)}), bf16[512,4,512]{0,2,1:T(8,128)(2,1)S(1)}, u32[]{:S(2)}, u32[]{:S(2)}) async-start(bf16[512,4,512]{0,2,1:T(8,128)(2,1)} %bitcast.32), calls=%async_computation | async-start | bytes 4194304 | tf_op jit(solution)/shard_map/all_to_all | solution.py:23
  16.9 0.0 reduce-scatter.2.cloned.1.call-start
  16.9 0.0 copy-done.2
  17.0 1.6 %collective-permute-start = (bf16[2048,128]{1,0:T(8,128)(2,1)S(1)}, bf16[2048,128]{1,0:T(8,128)(2,1)S(1)}, u32[]{:S(2)}, u32[]{:S(2)}) collective-permute-start(bf16[2048,128]{1,0:T(8,128)(2,1)S(1)} %copy-done.2), channel_id=1, source_target_pairs={{16,0},{0,16},{17,1},{1,17},{18,2},{2,18},{19,3},{3,19},{20,4},{4,... | collective-permute-start | bytes 1572872 | tf_op jit(solution)/shard_map/ppermute | solution.py:10
  18.5 0.0 copy-done.6
  18.5 0.0 copy-done.5
  18.5 0.5 select_reduce_fusion.2
  19.0 0.0 copy-done.3
  19.0 4.4 %select_reduce_fusion = (s32[2048]{0:T(1024)S(1)}, s32[2048]{0:T(1024)S(1)}) fusion(s32[2048]{0:T(1024)S(1)} %bitcast.38, s32[1600]{0:T(1024)S(1)} %copy-done.5, s32[2048]{0:T(1024)S(1)} %bitcast.37), kind=kLoop, calls=%fused_computation | loop fusion | flops 19656704 | bytes 39168 | tf_op jit(solution)/shard_map/reduce_sum | solution.py:15
  23.5 0.1 constant_dynamic-slice_fusion
  23.6 0.1 fusion.13
  23.6 41.5 %all-to-all-done = bf16[512,4,512]{0,2,1:T(8,128)(2,1)S(1)} async-done(((bf16[512,4,512]{0,2,1:T(8,128)(2,1)}), bf16[512,4,512]{0,2,1:T(8,128)(2,1)S(1)}, u32[]{:S(2)}, u32[]{:S(2)}) %all-to-all-start) | async-done | bytes 2097184 | tf_op jit(solution)/shard_map/all_to_all | solution.py:23
  65.1 0.0 copy-start
  65.1 1.3 %copy-done = bf16[512,4,512]{0,2,1:T(8,128)(2,1)} copy-done((bf16[512,4,512]{0,2,1:T(8,128)(2,1)}, bf16[512,4,512]{0,2,1:T(8,128)(2,1)S(1)}, u32[]{:S(2)}) %copy-start) | copy-done | bytes 2097176
  66.5 2.8 %copy.13 = bf16[4,512,512]{2,1,0:T(8,128)(2,1)S(1)} copy(bf16[4,512,512]{1,2,0:T(8,128)(2,1)} %bitcast.31) | data formatting | bytes 4194304 | tf_op jit(solution)/shard_map/all_to_all | solution.py:23
  69.3 1.0 fusion.1
  70.3 0.0 copy-start.4
  70.3 0.0 copy-start.7
  70.3 0.0 copy-start.8
  70.3 0.0 collective-permute-done
  70.3 1.0 fusion
  71.3 0.0 copy-start.1
  71.3 0.7 copy-done.1
  72.0 0.0 reduce-scatter.2.cloned.1.call-update
  72.1 0.0 copy-done.4
  72.1 0.3 select_reduce_fusion.6
  72.3 0.0 copy-done.7
  72.3 0.0 copy-done.8
  72.4 0.3 select_reduce_fusion.4
  72.7 18.7 %reduce-scatter.2.cloned.1.call-done = bf16[512,64]{0,1:T(8,128)(2,1)} async-done(((bf16[512,256]{0,1:T(8,128)(2,1)}), bf16[512,64]{0,1:T(8,128)(2,1)}) %reduce-scatter.2.cloned.1.call-update) | async-done | bytes 65552 | tf_op jit(solution)/shard_map/reduce_scatter | solution.py:52
  91.3 0.9 divide_convert_fusion
  92.3 10.2 %all_to_all.38 = bf16[4,16,512]{2,1,0:T(8,128)(2,1)S(1)} all-to-all(bf16[4,16,512]{2,1,0:T(8,128)(2,1)S(1)} %bitcast.33), channel_id=1, replica_groups=mesh['blk'=2,'wide'=4,'rep'=4] {'wide'}, dimensions={0} | all-to-all | bytes 131072 | tf_op jit(solution)/shard_map/all_to_all | solution.py:61
  102.4 0.6 copy.15
  (9 shorter events, 0.1 us)
Async XLA Ops:
  10.5 6.5 %copy-start.2 = (bf16[2048,128]{1,0:T(8,128)(2,1)S(1)}, bf16[2048,128]{1,0:T(8,128)(2,1)}, u32[]{:S(2)}) copy-start(bf16[2048,128]{1,0:T(8,128)(2,1)} %param.9) | copy-start | bytes 1572868
  10.5 8.0 %copy-start.6 = (s32[256,2]{0,1:T(2,128)S(1)}, s32[256,2]{0,1:T(2,128)}, u32[]{:S(2)}) copy-start(s32[256,2]{0,1:T(2,128)} %param.14) | copy-start | bytes 6148
  10.5 8.0 %copy-start.5 = (s32[1600]{0:T(1024)S(1)}, s32[1600]{0:T(1024)}, u32[]{:S(2)}) copy-start(s32[1600]{0:T(1024)} %param.12) | copy-start | bytes 19204
  10.5 8.5 %copy-start.3 = (s32[2048,2]{0,1:T(2,128)S(1)}, s32[2048,2]{0,1:T(2,128)}, u32[]{:S(2)}) copy-start(s32[2048,2]{0,1:T(2,128)} %param.15) | copy-start | bytes 49156
  10.5 54.7 %all-to-all-start = ((bf16[512,4,512]{0,2,1:T(8,128)(2,1)}), bf16[512,4,512]{0,2,1:T(8,128)(2,1)S(1)}, u32[]{:S(2)}, u32[]{:S(2)}) async-start(bf16[512,4,512]{0,2,1:T(8,128)(2,1)} %bitcast.32), calls=%async_computation | async-start | bytes 4194304 | tf_op jit(solution)/shard_map/all_to_all | solution.py:23
  16.9 74.4 %reduce-scatter.2.cloned.1.call-start = ((), (), s32[]{:S(2)}) async-start(), calls=%async_computation.3 | async-start | bytes 327680 | tf_op jit(solution)/shard_map/reduce_scatter | solution.py:52
  17.0 53.4 %collective-permute-start = (bf16[2048,128]{1,0:T(8,128)(2,1)S(1)}, bf16[2048,128]{1,0:T(8,128)(2,1)S(1)}, u32[]{:S(2)}, u32[]{:S(2)}) collective-permute-start(bf16[2048,128]{1,0:T(8,128)(2,1)S(1)} %copy-done.2), channel_id=1, source_target_pairs={{16,0},{0,16},{17,1},{1,17},{18,2},{2,18},{19,3},{3,19},{20,4},{4,... | collective-permute-start | bytes 1572872 | tf_op jit(solution)/shard_map/ppermute | solution.py:10
  65.1 1.4 %copy-start = (bf16[512,4,512]{0,2,1:T(8,128)(2,1)}, bf16[512,4,512]{0,2,1:T(8,128)(2,1)S(1)}, u32[]{:S(2)}) copy-start(bf16[512,4,512]{0,2,1:T(8,128)(2,1)S(1)} %all-to-all-done) | copy-start | bytes 6291460
  70.3 1.8 %copy-start.4 = (f32[1600]{0:T(1024)S(1)}, f32[1600]{0:T(1024)}, u32[]{:S(2)}) copy-start(f32[1600]{0:T(1024)} %param.11) | copy-start | bytes 19204
  70.3 2.0 %copy-start.7 = (s32[512,2]{0,1:T(2,128)S(1)}, s32[512,2]{0,1:T(2,128)}, u32[]{:S(2)}) copy-start(s32[512,2]{0,1:T(2,128)} %param.13) | copy-start | bytes 12292
  70.3 2.0 %copy-start.8 = (f32[400]{0:T(512)S(1)}, f32[400]{0:T(512)}, u32[]{:S(2)}) copy-start(f32[400]{0:T(512)} %param.10) | copy-start | bytes 4804
  71.3 0.7 copy-start.1
Sparse Core Ops, SparseCore 0:
  72.2 19.1 reduce-scatter.1
where the time goes:
time: 110 us
  waiting for transfers between devices  60.2 us (55%)
  between operations  13.6 us (12%)
  blocking collectives  10.2 us (9%)
  local copies, waits for them, and re-layouts  9.63 us (9%)
  starting transfers between devices  8.02 us (7%)
  other arithmetic  6.35 us (6%)
  matrix products  1.95 us (2%)
    all_to_all x1, waiting for transfers between devices, per_device(): lax.all_to_all(amplitudes, 'wide', split_axis=1, concat_axis=0, tiled=True)  41.5 us
    reduce_scatter x1, waiting for transfers between devices, per_device(): lax.psum_scatter(partial_value.astype(jnp.bfloat16), 'rep', scatter_dimen...  18.7 us
    all_to_all x1, blocking collectives, per_device(): lax.all_to_all(updated.T, 'wide', split_axis=0, concat_axis=1, tiled=True)  10.2 us
    all_to_all x1, starting transfers between devices, per_device(): lax.all_to_all(amplitudes, 'wide', split_axis=1, concat_axis=0, tiled=True)  6.46 us
    unnamed x19, local copies, waits for them, and re-layouts  6.01 us
    reduce_sum x4, other arithmetic, lookup(): jnp.sum(jnp.where(matched, source_table[None, :], jnp.zeros_like(source_t...  5.4 us
    all_to_all x1, local copies, waits for them, and re-layouts, per_device(): lax.all_to_all(amplitudes, 'wide', split_axis=1, concat_axis=0, tiled=True)  2.79 us
  transfers between devices with their start and end apart: 3, of which 2 were waited for; matrix products, arithmetic and copies ran while one was open for 9% of the time, Pallas kernels for 0%

commit v1 on v0

--- a/solution.py
+++ b/solution.py
@@ -1,7 +1,258 @@
 import jax
 import jax.numpy as jnp
 from jax import lax
+from jax.experimental import pallas as pl
+from jax.experimental.pallas import tpu as pltpu
 from jax.sharding import PartitionSpec as P
+
+MESH = pl.DeviceIdType.MESH
+DEPTH = 256
+
+
+def three_parts(values):
+    high = values.astype(jnp.bfloat16).astype(jnp.float32)
+    rest = values - high
+    middle = rest.astype(jnp.bfloat16).astype(jnp.float32)
+    return high, middle, rest - middle
+
+
+def as_rows(rows, extent):
+    row = lax.broadcasted_iota(jnp.int32, (16, extent), 0)
+    table = jnp.zeros((16, extent), jnp.float32)
+    for place, values in enumerate(rows):
+        table = jnp.where(row == place, values, table)
+    return table.astype(jnp.bfloat16)
+
+
+def pair_sums(table_ref, first, second):
+    extent = table_ref.shape[1]
+    pairs = first.shape[1]
+    total = jnp.zeros((16, pairs), jnp.float32)
+    for start in range(0, extent, DEPTH):
+        size = min(DEPTH, extent - start)
+        orbital = lax.broadcasted_iota(jnp.int32, (size, pairs), 0) + start
+        count = jnp.where(orbital == first, 1.0, 0.0) + jnp.where(orbital == second, 1.0, 0.0)
+        total += jnp.dot(
+            table_ref[:, start:start + size],
+            count.astype(jnp.bfloat16),
+            preferred_element_type=jnp.float32,
+        )
+    return total
+
+
+def labels_of(sums):
+    low = jnp.where(sums[0:1] == 2.0, 0.0, sums[0:1])
+    high = jnp.where(sums[1:2] == 2.0, 0.0, sums[1:2])
+    return low + 2.0 * high
+
+
+def ladder_kernel(
+    amp_ref, int_ref, occ_ref, virt_ref, irrep_ref, ij_ref, ab_ref, cd_ref, out_ref,
+    amp_v, own_v, peer_v, virt_tab, occ_tab, ab_lab, virt_col, occ_all,
+    part, part_in, half, half_in, tile, tile_in,
+    load_sem, x_sem, core_sem, y_sem, z_sem, occ_sem,
+):
+    n_chunk, depth, width = amp_v.shape
+    n_wide, rows = tile.shape[1], tile.shape[2]
+    cols = own_v.shape[1]
+    group = half.shape[2]
+    b, w, r = lax.axis_index("blk"), lax.axis_index("wide"), lax.axis_index("rep")
+    y, c = r // 2, r % 2
+    other_b = 1 - b
+    sibling = y * 2 + (1 - c)
+    across = (1 - y) * 2 + c
+    send_step = (b + y + 1) % 2
+    keep_step = 1 - send_step
+    wides = [(w + k) % n_wide for k in range(n_wide)]
+
+    my_rows = pl.ds(pl.multiple_of(w * depth, depth), depth)
+    own_load = pltpu.make_async_copy(int_ref.at[my_rows, :], own_v, load_sem.at[n_chunk])
+    own_load.start()
+    amp_loads = []
+    for j in range(n_chunk):
+        load = pltpu.make_async_copy(
+            amp_ref.at[:, pl.ds(j * width, width)], amp_v.at[j], load_sem.at[j]
+        )
+        load.start()
+        amp_loads.append(load)
+
+    barrier = pltpu.get_barrier_semaphore()
+    partners = [{"blk": other_b}, {"rep": sibling}, {"rep": across}]
+    partners += [{"wide": wides[k]} for k in range(1, n_wide)]
+    for partner in partners:
+        pl.semaphore_signal(barrier, inc=1, device_id=partner, device_id_type=MESH)
+    pl.semaphore_wait(barrier, len(partners))
+
+    def remote(src, dst, sems, place, partner):
+        return pltpu.make_async_remote_copy(
+            src_ref=src,
+            dst_ref=dst,
+            send_sem=sems.at[(0,) + place],
+            recv_sem=sems.at[(1,) + place],
+            device_id=partner,
+            device_id_type=MESH,
+        )
+
+    x_copy = remote(int_ref.at[my_rows, :], peer_v, x_sem, (0,), {"blk": other_b})
+    x_copy.start()
+
+    n_virt, n_occ = virt_ref.shape[0], occ_ref.shape[0]
+    irrep = irrep_ref[...].reshape(1, n_virt)
+    energies = three_parts(virt_ref[...].reshape(1, n_virt))
+    bits = ((irrep & 1).astype(jnp.float32), ((irrep >> 1) & 1).astype(jnp.float32))
+    virt_tab[...] = as_rows(bits + energies, n_virt)
+    occ_tab[...] = as_rows(three_parts(occ_ref[...].reshape(1, n_occ)), n_occ)
+
+    my_lanes = pl.ds(pl.multiple_of(w * depth, depth), depth)
+    cd_sums = pair_sums(virt_tab, cd_ref[0:1, my_lanes], cd_ref[1:2, my_lanes])
+    cd_label = jnp.broadcast_to(labels_of(cd_sums), (8, depth)).T[:, 0:1]
+    ab_sums = pair_sums(virt_tab, ab_ref[0:1, :], ab_ref[1:2, :])
+    ab_label = labels_of(ab_sums)
+    for h in range(2):
+        ab_lab[h] = jnp.broadcast_to(ab_label[:, h * cols:(h + 1) * cols], (8, cols))
+    pair_virt = (ab_sums[2:3] + ab_sums[3:4]) + ab_sums[4:5]
+    virt_col[...] = jnp.broadcast_to(pair_virt, (8, 2 * cols)).T
+
+    core_copies, y_copies = {}, {}
+
+    def contribute(step, slab_v, column):
+        kept = jnp.where(
+            cd_label == ab_lab[column][0:1], slab_v[...].astype(jnp.float32), 0.0
+        ).T.astype(jnp.bfloat16)
+        for j in range(n_chunk):
+            if step == 0:
+                amp_loads[j].wait()
+            product = jnp.dot(kept, amp_v[j], preferred_element_type=jnp.float32)
+            product = product.astype(jnp.bfloat16)
+            for core in range(2):
+                part[step, core, j] = product[core * group:(core + 1) * group]
+            copy = remote(
+                part.at[step, 1 - c, j], part_in.at[step, j], core_sem, (step, j), {"rep": sibling}
+            )
+            copy.start()
+            core_copies[step, j] = copy
+
+    def y_copy(j):
+        return remote(half.at[send_step, j], half_in.at[j], y_sem, (j,), {"rep": across})
+
+    def fold(step):
+        for j in range(n_chunk):
+            core_copies[step, j].wait()
+            half[step, j] = (
+                part[step, c, j].astype(jnp.float32) + part_in[step, j].astype(jnp.float32)
+            ).astype(jnp.bfloat16)
+
+            @pl.when(send_step == step)
+            def _():
+                y_copy(j).start()
+
+    own_load.wait()
+    contribute(0, own_v, b)
+    fold(0)
+
+    occ_sums = pair_sums(occ_tab, ij_ref[0:1, :], ij_ref[1:2, :])
+    pair_occ = (occ_sums[0:1] + occ_sums[1:2]) + occ_sums[2:3]
+    occ_all[w] = jnp.broadcast_to(pair_occ, (8, width))
+    occ_copies = [
+        remote(occ_all.at[w], occ_all.at[w], occ_sem, (k,), {"wide": wides[k]})
+        for k in range(1, n_wide)
+    ]
+    for copy in occ_copies:
+        copy.start()
+
+    x_copy.wait()
+    contribute(1, peer_v, other_b)
+    fold(1)
+
+    z_copies = {}
+    for j in range(n_chunk):
+        y_copy(j).wait()
+        total = half[keep_step, j].astype(jnp.float32) + half_in[j].astype(jnp.float32)
+        total = total.astype(jnp.bfloat16)
+        for i in range(n_wide):
+            tile[j, i] = total[i * rows:(i + 1) * rows]
+        for k in range(1, n_wide):
+            copy = remote(
+                tile.at[j, wides[k]], tile_in.at[j, k], z_sem, (j, k), {"wide": wides[k]}
+            )
+            copy.start()
+            z_copies[j, k] = copy
+
+    for copy in occ_copies:
+        copy.wait()
+    my_virt = virt_col[pl.ds(pl.multiple_of(r * group + w * rows, rows), rows), :][:, 0:1]
+    for j in range(n_chunk):
+        ladder = tile[j, w].astype(jnp.float32)
+        for k in range(1, n_wide):
+            z_copies[j, k].wait()
+            ladder += tile_in[j, k].astype(jnp.float32)
+        out_ref[:, j * width:(j + 1) * width] = (
+            ladder / (occ_all[j][0:1] - my_virt)
+        ).astype(jnp.bfloat16)
+
+
+def in_place(
+    amplitudes, integrals, occ_energy, virt_energy, virt_irrep, ij_pairs, ab_pairs, cd_pairs
+):
+    depth, n_ij = amplitudes.shape
+    cols = integrals.shape[1]
+    n_ab = ab_pairs.shape[0]
+    n_wide, n_rep = lax.axis_size("wide"), lax.axis_size("rep")
+    width = ij_pairs.shape[0]
+    group = n_ab // n_rep
+    rows = group // n_wide
+    bf16, f32 = jnp.bfloat16, jnp.float32
+    vmem, hbm = pl.BlockSpec(memory_space=pltpu.VMEM), pl.BlockSpec(memory_space=pl.ANY)
+    dma = pltpu.SemaphoreType.DMA
+    return pl.pallas_call(
+        ladder_kernel,
+        out_shape=jax.ShapeDtypeStruct((rows, n_ij), bf16),
+        in_specs=[hbm, hbm] + [vmem] * 6,
+        out_specs=vmem,
+        scratch_shapes=[
+            pltpu.VMEM((n_wide, depth, width), bf16),
+            pltpu.VMEM((depth, cols), bf16),
+            pltpu.VMEM((depth, cols), bf16),
+            pltpu.VMEM((16, virt_energy.shape[0]), bf16),
+            pltpu.VMEM((16, occ_energy.shape[0]), bf16),
+            pltpu.VMEM((2, 8, cols), f32),
+            pltpu.VMEM((n_ab, 8), f32),
+            pltpu.VMEM((n_wide, 8, width), f32),
+            pltpu.VMEM((2, 2, n_wide, group, width), bf16),
+            pltpu.VMEM((2, n_wide, group, width), bf16),
+            pltpu.VMEM((2, n_wide, group, width), bf16),
+            pltpu.VMEM((n_wide, group, width), bf16),
+            pltpu.VMEM((n_wide, n_wide, rows, width), bf16),
+            pltpu.VMEM((n_wide, n_wide, rows, width), bf16),
+            dma((n_wide + 1,)),
+            dma((2, 1)),
+            dma((2, 2, n_wide)),
+            dma((2, n_wide)),
+            dma((2, n_wide, n_wide)),
+            dma((2, n_wide)),
+        ],
+        compiler_params=pltpu.CompilerParams(
+            collective_id=0, has_side_effects=True, vmem_limit_bytes=32 * 1024 * 1024
+        ),
+        name="ladder",
+    )(amplitudes, integrals, occ_energy, virt_energy, virt_irrep, ij_pairs.T, ab_pairs.T, cd_pairs.T)
+
+
+def fits_in_place(amplitudes, integrals, ij_pairs, ab_pairs):
+    n_blk, n_wide, n_rep = (lax.axis_size(axis) for axis in ("blk", "wide", "rep"))
+    n_ab, n_ij = ab_pairs.shape[0], amplitudes.shape[1]
+    return (
+        n_blk == 2
+        and n_rep == 4
+        and integrals.shape[1] * 2 == n_ab
+        and integrals.shape[1] % 128 == 0
+        and n_ab % (n_rep * n_wide * 16) == 0
+        and ij_pairs.shape[0] * n_wide == n_ij
+        and ij_pairs.shape[0] % 128 == 0
+        and amplitudes.shape[0] % 128 == 0
+        and n_ab * n_ij <= 2**20
+        and amplitudes.size <= 2**21
+    )
 
 
 def passed_along(block, axis, distance):
@@ -17,7 +268,7 @@
     )
 
 
-def per_device(
+def gathered(
     amplitudes, integrals, occ_energy, virt_energy, virt_irrep, ij_pairs, ab_pairs, cd_pairs
 ):
     amp_rows = lax.all_to_all(amplitudes, "wide", split_axis=1, concat_axis=0, tiled=True)
@@ -61,6 +312,15 @@
     return lax.all_to_all(updated.T, "wide", split_axis=0, concat_axis=1, tiled=True)
 
 
+def per_device(
+    amplitudes, integrals, occ_energy, virt_energy, virt_irrep, ij_pairs, ab_pairs, cd_pairs
+):
+    plan = in_place if fits_in_place(amplitudes, integrals, ij_pairs, ab_pairs) else gathered
+    return plan(
+        amplitudes, integrals, occ_energy, virt_energy, virt_irrep, ij_pairs, ab_pairs, cd_pairs
+    )
+
+
 def solution(mesh):
     in_specs = (
         P(("rep", "wide"), "blk"),

time: 110 us -> 29.6 us (0.27)
  waiting for transfers between devices: 60.2 us -> 0 us
  Pallas kernels: 0 us -> 21.7 us
  between operations: 13.6 us -> 0.02 us
  blocking collectives: 10.2 us -> 0 us
  starting transfers between devices: 8.02 us -> 0 us
  other arithmetic: 6.35 us -> 0 us
  local copies, waits for them, and re-layouts: 9.63 us -> 7.42 us
  matrix products: 1.95 us -> 0 us
    all_to_all x1 -> x0, waiting for transfers between devices: 41.5 us -> none  [per_device(): lax.all_to_all(amplitudes, 'wide', split_axis=1, concat_axis=0, tiled=True)]
    pallas_call x0 -> x1, Pallas kernels: none -> 21.7 us  [in_place(): pl.pallas_call(ladder_kernel, out_shape=jax.ShapeDtypeStruct((rows, n_ij)...]
    reduce_scatter x1 -> x0, waiting for transfers between devices: 18.7 us -> none  [per_device(): lax.psum_scatter(partial_value.astype(jnp.bfloat16), 'rep', scatter_dimen...]
    all_to_all x1 -> x0, blocking collectives: 10.2 us -> none  [per_device(): lax.all_to_all(updated.T, 'wide', split_axis=0, concat_axis=1, tiled=True)]
    all_to_all x1 -> x0, starting transfers between devices: 6.46 us -> none  [per_device(): lax.all_to_all(amplitudes, 'wide', split_axis=1, concat_axis=0, tiled=True)]
    reduce_sum x4 -> x0, other arithmetic: 5.4 us -> none  [lookup(): jnp.sum(jnp.where(matched, source_table[None, :], jnp.zeros_like(source_t...]
    all_to_all x2 -> x0, local copies, waits for them, and re-layouts: 3.42 us -> none  [the longest x1 2.79 us: per_device(): lax.all_to_all(amplitudes, 'wide', split_axis=1, concat_axis=0, tiled=True)]
    dot_general x2 -> x0, matrix products: 1.95 us -> none  [per_device(): lax.dot_general(amp_rows, masked, (((0,), (0,)), ((), ())), preferred_ele...]
  transfers between devices with their start and end apart: 3 -> 0, of which waited for: 2 -> 0; matrix products, arithmetic and copies ran while one was open for 9% -> 0% of each run, Pallas kernels for 0% -> 0%
where the time goes in v1:
time: 29.6 us; the launch traced here: 29.1 us
  Pallas kernels  21.7 us (73%)
  local copies, waits for them, and re-layouts  7.42 us (25%)
    pallas_call x1, Pallas kernels, in_place(): pl.pallas_call(ladder_kernel, out_shape=jax.ShapeDtypeStruct((rows, n_ij)...  21.7 us
    unnamed x17, local copies, waits for them, and re-layouts  7.42 us

profile of v1, /device:TPU:0, one launch (start us, length us, event | category | flops | bytes accessed | tf_op | source)
XLA Modules:
  0.0 29.1 jit_solution(6810321056859399511)
XLA Ops:
  0.0 0.0 copy-start
  0.0 1.6 %copy-done = bf16[512,2048]{1,0:T(8,128)(2,1)S(1)} copy-done((bf16[512,2048]{1,0:T(8,128)(2,1)S(1)}, bf16[512,2048]{1,0:T(8,128)(2,1)}, u32[]{:S(2)}) %copy-start) | copy-done | bytes 2097176
  1.6 0.0 copy-start.1
  1.6 1.0 %copy-done.1 = bf16[2048,128]{1,0:T(8,128)(2,1)S(1)} copy-done((bf16[2048,128]{1,0:T(8,128)(2,1)S(1)}, bf16[2048,128]{1,0:T(8,128)(2,1)}, u32[]{:S(2)}) %copy-start.1) | copy-done | bytes 524312
  2.6 0.0 copy-start.2
  2.6 0.7 %copy-done.2 = s32[2048,2]{0,1:T(2,128)S(1)} copy-done((s32[2048,2]{0,1:T(2,128)S(1)}, s32[2048,2]{0,1:T(2,128)}, u32[]{:S(2)}) %copy-start.2) | copy-done | bytes 16408
  3.4 0.0 copy-start.3
  3.4 0.7 %copy-done.3 = f32[1600]{0:T(1024)S(1)} copy-done((f32[1600]{0:T(1024)S(1)}, f32[1600]{0:T(1024)}, u32[]{:S(2)}) %copy-start.3) | copy-done | bytes 6424
  4.0 0.0 copy-start.4
  4.1 0.7 %copy-done.4 = s32[1600]{0:T(1024)S(1)} copy-done((s32[1600]{0:T(1024)S(1)}, s32[1600]{0:T(1024)}, u32[]{:S(2)}) %copy-start.4) | copy-done | bytes 6424
  4.7 0.0 copy-start.5
  4.7 0.7 %copy-done.5 = s32[512,2]{0,1:T(2,128)S(1)} copy-done((s32[512,2]{0,1:T(2,128)S(1)}, s32[512,2]{0,1:T(2,128)}, u32[]{:S(2)}) %copy-start.5) | copy-done | bytes 4120
  5.4 0.0 copy-start.6
  5.4 0.7 %copy-done.6 = f32[400]{0:T(512)S(1)} copy-done((f32[400]{0:T(512)S(1)}, f32[400]{0:T(512)}, u32[]{:S(2)}) %copy-start.6) | copy-done | bytes 1624
  6.1 0.0 copy-start.7
  6.1 0.7 %copy-done.7 = s32[256,2]{0,1:T(2,128)S(1)} copy-done((s32[256,2]{0,1:T(2,128)S(1)}, s32[256,2]{0,1:T(2,128)}, u32[]{:S(2)}) %copy-start.7) | copy-done | bytes 2072
  6.8 21.7 %ladder.1 = bf16[16,2048]{1,0:T(8,128)(2,1)S(1)} custom-call(bf16[512,2048]{1,0:T(8,128)(2,1)S(1)} %copy-done, bf16[2048,128]{1,0:T(8,128)(2,1)S(1)} %copy-done.1, f32[400]{0:T(512)S(1)} %copy-done.6, f32[1600]{0:T(1024)S(1)} %copy-done.3, s32[1600]{0:T(1024)S(1)} %copy-done.4, s32[2,512]{1,0:T(2,128)S(1)} %bitcast.4, s32[2,256]{1,0:T(2,128)S(1)} %bitcast.5, ...), custom_call_target="tpu_custom_call" | custom-call | tf_op jit(solution)/shard_map/ladder/pallas_call | solution.py:207
  28.5 0.6 %copy.10 = bf16[16,2048]{1,0:T(8,128)(2,1)} copy(bf16[16,2048]{1,0:T(8,128)(2,1)S(1)} %ladder.1) | data formatting | bytes 131072
Async XLA Ops:
  0.0 1.6 %copy-start = (bf16[512,2048]{1,0:T(8,128)(2,1)S(1)}, bf16[512,2048]{1,0:T(8,128)(2,1)}, u32[]{:S(2)}) copy-start(bf16[512,2048]{1,0:T(8,128)(2,1)} %amp_ref.1) | copy-start | bytes 6291460
  1.6 1.0 %copy-start.1 = (bf16[2048,128]{1,0:T(8,128)(2,1)S(1)}, bf16[2048,128]{1,0:T(8,128)(2,1)}, u32[]{:S(2)}) copy-start(bf16[2048,128]{1,0:T(8,128)(2,1)} %int_ref.1) | copy-start | bytes 1572868
  2.6 0.7 %copy-start.2 = (s32[2048,2]{0,1:T(2,128)S(1)}, s32[2048,2]{0,1:T(2,128)}, u32[]{:S(2)}) copy-start(s32[2048,2]{0,1:T(2,128)} %param.15) | copy-start | bytes 49156
  3.4 0.7 %copy-start.3 = (f32[1600]{0:T(1024)S(1)}, f32[1600]{0:T(1024)}, u32[]{:S(2)}) copy-start(f32[1600]{0:T(1024)} %virt_ref.1) | copy-start | bytes 19204
  4.0 0.7 %copy-start.4 = (s32[1600]{0:T(1024)S(1)}, s32[1600]{0:T(1024)}, u32[]{:S(2)}) copy-start(s32[1600]{0:T(1024)} %irrep_ref.1) | copy-start | bytes 19204
  4.7 0.7 %copy-start.5 = (s32[512,2]{0,1:T(2,128)S(1)}, s32[512,2]{0,1:T(2,128)}, u32[]{:S(2)}) copy-start(s32[512,2]{0,1:T(2,128)} %param.13) | copy-start | bytes 12292
  5.4 0.7 %copy-start.6 = (f32[400]{0:T(512)S(1)}, f32[400]{0:T(512)}, u32[]{:S(2)}) copy-start(f32[400]{0:T(512)} %occ_ref.1) | copy-start | bytes 4804
  6.1 0.7 %copy-start.7 = (s32[256,2]{0,1:T(2,128)S(1)}, s32[256,2]{0,1:T(2,128)}, u32[]{:S(2)}) copy-start(s32[256,2]{0,1:T(2,128)} %param.14) | copy-start | bytes 6148

commit v2 on v1

--- a/solution.py
+++ b/solution.py
@@ -47,8 +47,8 @@
 
 
 def ladder_kernel(
-    amp_ref, int_ref, occ_ref, virt_ref, irrep_ref, ij_ref, ab_ref, cd_ref, out_ref,
-    amp_v, own_v, peer_v, virt_tab, occ_tab, ab_lab, virt_col, occ_all,
+    amp_hbm, int_hbm, occ_hbm, virt_hbm, irrep_hbm, ij_hbm, ab_hbm, cd_hbm, out_ref,
+    occ_ref, virt_ref, irrep_ref, ij_ref, ab_ref, cd_ref, amp_v, own_v, peer_v, virt_tab, occ_tab, ab_lab, virt_col, occ_all,
     part, part_in, half, half_in, tile, tile_in,
     load_sem, x_sem, core_sem, y_sem, z_sem, occ_sem,
 ):
@@ -66,12 +66,23 @@
     wides = [(w + k) % n_wide for k in range(n_wide)]
 
     my_rows = pl.ds(pl.multiple_of(w * depth, depth), depth)
-    own_load = pltpu.make_async_copy(int_ref.at[my_rows, :], own_v, load_sem.at[n_chunk])
+    my_lanes = pl.ds(pl.multiple_of(w * depth, depth), depth)
+    small = [
+        (virt_hbm, virt_ref), (irrep_hbm, irrep_ref), (cd_hbm.at[:, my_lanes], cd_ref),
+        (ab_hbm, ab_ref), (occ_hbm, occ_ref), (ij_hbm, ij_ref),
+    ]
+    small_loads = [
+        pltpu.make_async_copy(src, dst, load_sem.at[n_chunk + 1 + place])
+        for place, (src, dst) in enumerate(small)
+    ]
+    for load in small_loads:
+        load.start()
+    own_load = pltpu.make_async_copy(int_hbm.at[my_rows, :], own_v, load_sem.at[n_chunk])
     own_load.start()
     amp_loads = []
     for j in range(n_chunk):
         load = pltpu.make_async_copy(
-            amp_ref.at[:, pl.ds(j * width, width)], amp_v.at[j], load_sem.at[j]
+            amp_hbm.at[:, pl.ds(j * width, width)], amp_v.at[j], load_sem.at[j]
         )
         load.start()
         amp_loads.append(load)
@@ -93,9 +104,11 @@
             device_id_type=MESH,
         )
 
-    x_copy = remote(int_ref.at[my_rows, :], peer_v, x_sem, (0,), {"blk": other_b})
+    x_copy = remote(int_hbm.at[my_rows, :], peer_v, x_sem, (0,), {"blk": other_b})
     x_copy.start()
 
+    for load in small_loads:
+        load.wait()
     n_virt, n_occ = virt_ref.shape[0], occ_ref.shape[0]
     irrep = irrep_ref[...].reshape(1, n_virt)
     energies = three_parts(virt_ref[...].reshape(1, n_virt))
@@ -103,8 +116,7 @@
     virt_tab[...] = as_rows(bits + energies, n_virt)
     occ_tab[...] = as_rows(three_parts(occ_ref[...].reshape(1, n_occ)), n_occ)
 
-    my_lanes = pl.ds(pl.multiple_of(w * depth, depth), depth)
-    cd_sums = pair_sums(virt_tab, cd_ref[0:1, my_lanes], cd_ref[1:2, my_lanes])
+    cd_sums = pair_sums(virt_tab, cd_ref[0:1, :], cd_ref[1:2, :])
     cd_label = jnp.broadcast_to(labels_of(cd_sums), (8, depth)).T[:, 0:1]
     ab_sums = pair_sums(virt_tab, ab_ref[0:1, :], ab_ref[1:2, :])
     ab_label = labels_of(ab_sums)
@@ -202,14 +214,21 @@
     group = n_ab // n_rep
     rows = group // n_wide
     bf16, f32 = jnp.bfloat16, jnp.float32
-    vmem, hbm = pl.BlockSpec(memory_space=pltpu.VMEM), pl.BlockSpec(memory_space=pl.ANY)
+    i32 = jnp.int32
+    vmem, hbm = pl.BlockSpec(memory_space=pltpu.VMEM), pl.BlockSpec(memory_space=pltpu.HBM)
     dma = pltpu.SemaphoreType.DMA
     return pl.pallas_call(
         ladder_kernel,
         out_shape=jax.ShapeDtypeStruct((rows, n_ij), bf16),
-        in_specs=[hbm, hbm] + [vmem] * 6,
+        in_specs=[hbm] * 8,
         out_specs=vmem,
         scratch_shapes=[
+            pltpu.VMEM(occ_energy.shape, f32),
+            pltpu.VMEM(virt_energy.shape, f32),
+            pltpu.VMEM(virt_irrep.shape, i32),
+            pltpu.VMEM((2, width), i32),
+            pltpu.VMEM((2, n_ab), i32),
+            pltpu.VMEM((2, depth), i32),
             pltpu.VMEM((n_wide, depth, width), bf16),
             pltpu.VMEM((depth, cols), bf16),
             pltpu.VMEM((depth, cols), bf16),
@@ -224,7 +243,7 @@
             pltpu.VMEM((n_wide, group, width), bf16),
             pltpu.VMEM((n_wide, n_wide, rows, width), bf16),
             pltpu.VMEM((n_wide, n_wide, rows, width), bf16),
-            dma((n_wide + 1,)),
+            dma((n_wide + 7,)),
             dma((2, 1)),
             dma((2, 2, n_wide)),
             dma((2, n_wide)),
@@ -232,7 +251,7 @@
             dma((2, n_wide)),
         ],
         compiler_params=pltpu.CompilerParams(
-            collective_id=0, has_side_effects=True, vmem_limit_bytes=32 * 1024 * 1024
+            collective_id=0, has_side_effects=True, vmem_limit_bytes=60 * 1024 * 1024
         ),
         name="ladder",
     )(amplitudes, integrals, occ_energy, virt_energy, virt_irrep, ij_pairs.T, ab_pairs.T, cd_pairs.T)

time: 29.6 us -> 23.8 us (0.80)
  local copies, waits for them, and re-layouts: 7.42 us -> 1.47 us
  Pallas kernels: 21.7 us -> 22.1 us
    unnamed x17 -> x1, local copies, waits for them, and re-layouts: 7.42 us -> 1.47 us
    pallas_call x1, Pallas kernels: 21.7 us -> 22.1 us  [in_place(): pl.pallas_call(ladder_kernel, out_shape=jax.ShapeDtypeStruct((rows, n_ij)...]
where the time goes in v2:
time: 23.8 us; the launch traced here: 23.6 us
  Pallas kernels  22.1 us (93%)
  local copies, waits for them, and re-layouts  1.47 us (6%)
    pallas_call x1, Pallas kernels, in_place(): pl.pallas_call(ladder_kernel, out_shape=jax.ShapeDtypeStruct((rows, n_ij)...  22.1 us
    unnamed x1, local copies, waits for them, and re-layouts  1.47 us

profile of v2, /device:TPU:0, one launch (start us, length us, event | category | flops | bytes accessed | tf_op | source)
XLA Modules:
  0.0 23.6 jit_solution(12831643025006773855)
XLA Ops:
  0.0 22.1 %ladder.1 = bf16[16,2048]{1,0:T(8,128)(2,1)} custom-call(bf16[512,2048]{1,0:T(8,128)(2,1)} %amp_hbm.1, bf16[2048,128]{1,0:T(8,128)(2,1)} %int_hbm.1, f32[400]{0:T(512)} %occ_hbm.1, f32[1600]{0:T(1024)} %virt_hbm.1, s32[1600]{0:T(1024)} %irrep_hbm.1, s32[2,512]{1,0:T(2,128)} %bitcast.4, s32[2,256]{1,0:T(2,128)} %bitcast.5, s32[2,2048]{1,0:T(2,128)} %bitcast.3), custom_call_target="tpu_custom_call" | custom-call | tf_op jit(solution)/shard_map/ladder/pallas_call | solution.py:220
  22.1 1.5 %copy.10 = bf16[16,2048]{1,0:T(8,128)(2,1)} copy(bf16[16,2048]{1,0:T(8,128)(2,1)} %ladder.1) | data formatting | bytes 131072

commit v3 on v2

--- a/solution.py
+++ b/solution.py
@@ -7,6 +7,8 @@
 
 MESH = pl.DeviceIdType.MESH
 DEPTH = 256
+LAG = 2
+Y_FIRST = ((0, 2), (0, 1, 2))
 
 
 def three_parts(values):
@@ -49,8 +51,8 @@
 def ladder_kernel(
     amp_hbm, int_hbm, occ_hbm, virt_hbm, irrep_hbm, ij_hbm, ab_hbm, cd_hbm, out_ref,
     occ_ref, virt_ref, irrep_ref, ij_ref, ab_ref, cd_ref, amp_v, own_v, peer_v, virt_tab, occ_tab, ab_lab, virt_col, occ_all,
-    part, part_in, half, half_in, tile, tile_in,
-    load_sem, x_sem, core_sem, y_sem, z_sem, occ_sem,
+    part, part_in, half, half_in, tile, tile_in, early, early_in, slim, slim_in,
+    load_sem, x_sem, core_sem, y_sem, z_sem, early_sem, slim_sem, occ_sem,
 ):
     n_chunk, depth, width = amp_v.shape
     n_wide, rows = tile.shape[1], tile.shape[2]
@@ -62,7 +64,6 @@
     sibling = y * 2 + (1 - c)
     across = (1 - y) * 2 + c
     send_step = (b + y + 1) % 2
-    keep_step = 1 - send_step
     wides = [(w + k) % n_wide for k in range(n_wide)]
 
     my_rows = pl.ds(pl.multiple_of(w * depth, depth), depth)
@@ -125,7 +126,9 @@
     pair_virt = (ab_sums[2:3] + ab_sums[3:4]) + ab_sums[4:5]
     virt_col[...] = jnp.broadcast_to(pair_virt, (8, 2 * cols)).T
 
-    core_copies, y_copies = {}, {}
+    core_copies = {}
+    y_first = [[j for j in range(n_chunk) if j % 4 in some] for some in Y_FIRST]
+    z_first = [[j for j in range(n_chunk) if j % 4 not in some] for some in Y_FIRST]
 
     def contribute(step, slab_v, column):
         kept = jnp.where(
@@ -143,24 +146,51 @@
             )
             copy.start()
             core_copies[step, j] = copy
+            if j >= LAG:
+                fold(step, j - LAG)
+        for j in range(max(n_chunk - LAG, 0), n_chunk):
+            fold(step, j)
 
     def y_copy(j):
         return remote(half.at[send_step, j], half_in.at[j], y_sem, (j,), {"rep": across})
 
-    def fold(step):
-        for j in range(n_chunk):
-            core_copies[step, j].wait()
-            half[step, j] = (
-                part[step, c, j].astype(jnp.float32) + part_in[step, j].astype(jnp.float32)
-            ).astype(jnp.bfloat16)
+    def slim_copy(j):
+        return remote(slim.at[j], slim_in.at[j], slim_sem, (j,), {"rep": across})
+
+    def early_copy(step, j, k):
+        return remote(
+            early.at[step, j, wides[k]], early_in.at[step, j, k], early_sem, (step, j, k),
+            {"wide": wides[k]},
+        )
+
+    def fold(step, j):
+        core_copies[step, j].wait_recv()
+        total = (
+            part[step, c, j].astype(jnp.float32) + part_in[step, j].astype(jnp.float32)
+        ).astype(jnp.bfloat16)
+        if j in y_first[step]:
+            half[step, j] = total
 
             @pl.when(send_step == step)
             def _():
                 y_copy(j).start()
+        else:
+            for i in range(n_wide):
+                early[step, j, i] = total[i * rows:(i + 1) * rows]
+            for k in range(1, n_wide):
+                early_copy(step, j, k).start()
+
+    def wide_sum(step, j):
+        ladder = early[step, j, w].astype(jnp.float32)
+        for k in range(1, n_wide):
+            early_copy(step, j, k).wait_recv()
+            ladder += early_in[step, j, k].astype(jnp.float32)
+        return ladder
 
     own_load.wait()
     contribute(0, own_v, b)
-    fold(0)
+    x_copy.wait_recv()
+    contribute(1, peer_v, other_b)
 
     occ_sums = pair_sums(occ_tab, ij_ref[0:1, :], ij_ref[1:2, :])
     pair_occ = (occ_sums[0:1] + occ_sums[1:2]) + occ_sums[2:3]
@@ -172,35 +202,71 @@
     for copy in occ_copies:
         copy.start()
 
-    x_copy.wait()
-    contribute(1, peer_v, other_b)
-    fold(1)
-
-    z_copies = {}
-    for j in range(n_chunk):
-        y_copy(j).wait()
-        total = half[keep_step, j].astype(jnp.float32) + half_in[j].astype(jnp.float32)
-        total = total.astype(jnp.bfloat16)
-        for i in range(n_wide):
-            tile[j, i] = total[i * rows:(i + 1) * rows]
-        for k in range(1, n_wide):
-            copy = remote(
-                tile.at[j, wides[k]], tile_in.at[j, k], z_sem, (j, k), {"wide": wides[k]}
-            )
-            copy.start()
-            z_copies[j, k] = copy
+    def z_copy(j, k):
+        return remote(
+            tile.at[j, wides[k]], tile_in.at[j, k], z_sem, (j, k), {"wide": wides[k]}
+        )
+
+    def spread(step):
+        for j in y_first[step]:
+            y_copy(j).wait_recv()
+            total = half[step, j].astype(jnp.float32) + half_in[j].astype(jnp.float32)
+            total = total.astype(jnp.bfloat16)
+            for i in range(n_wide):
+                tile[j, i] = total[i * rows:(i + 1) * rows]
+            for k in range(1, n_wide):
+                z_copy(j, k).start()
+
+    def cross(step):
+        for j in z_first[step]:
+            slim[j] = wide_sum(step, j).astype(jnp.bfloat16)
+            slim_copy(j).start()
+
+    @pl.when(send_step == 1)
+    def _():
+        spread(0)
+        cross(1)
+
+    @pl.when(send_step == 0)
+    def _():
+        cross(0)
+        spread(1)
 
     for copy in occ_copies:
-        copy.wait()
+        copy.wait_recv()
     my_virt = virt_col[pl.ds(pl.multiple_of(r * group + w * rows, rows), rows), :][:, 0:1]
-    for j in range(n_chunk):
-        ladder = tile[j, w].astype(jnp.float32)
-        for k in range(1, n_wide):
-            z_copies[j, k].wait()
-            ladder += tile_in[j, k].astype(jnp.float32)
+
+    def finish(j, ladder):
         out_ref[:, j * width:(j + 1) * width] = (
             ladder / (occ_all[j][0:1] - my_virt)
         ).astype(jnp.bfloat16)
+
+    def gather(step):
+        for j in z_first[step]:
+            ladder = wide_sum(step, j)
+            slim_copy(j).wait_recv()
+            finish(j, ladder + slim_in[j].astype(jnp.float32))
+        for j in y_first[step]:
+            ladder = tile[j, w].astype(jnp.float32)
+            for k in range(1, n_wide):
+                z_copy(j, k).wait_recv()
+                ladder += tile_in[j, k].astype(jnp.float32)
+            finish(j, ladder)
+
+    def leave(copies):
+        for copy in copies:
+            copy.wait_send()
+
+    for step in range(2):
+        @pl.when(send_step == 1 - step)
+        def _():
+            gather(step)
+            leave([y_copy(j) for j in y_first[1 - step]])
+            leave([slim_copy(j) for j in z_first[1 - step]])
+            leave([z_copy(j, k) for j in y_first[step] for k in range(1, n_wide)])
+
+        leave([early_copy(step, j, k) for j in z_first[step] for k in range(1, n_wide)])
+    leave([x_copy] + occ_copies + list(core_copies.values()))
 
 
 def in_place(
@@ -243,11 +309,17 @@
             pltpu.VMEM((n_wide, group, width), bf16),
             pltpu.VMEM((n_wide, n_wide, rows, width), bf16),
             pltpu.VMEM((n_wide, n_wide, rows, width), bf16),
+            pltpu.VMEM((2, n_wide, n_wide, rows, width), bf16),
+            pltpu.VMEM((2, n_wide, n_wide, rows, width), bf16),
+            pltpu.VMEM((n_wide, rows, width), bf16),
+            pltpu.VMEM((n_wide, rows, width), bf16),
             dma((n_wide + 7,)),
             dma((2, 1)),
             dma((2, 2, n_wide)),
             dma((2, n_wide)),
             dma((2, n_wide, n_wide)),
+            dma((2, 2, n_wide, n_wide)),
+            dma((2, n_wide)),
             dma((2, n_wide)),
         ],
         compiler_params=pltpu.CompilerParams(

time: 23.8 us -> 22.8 us (0.958)
  Pallas kernels: 22.1 us -> 21.2 us
    pallas_call x1, Pallas kernels: 22.1 us -> 21.2 us  [in_place(): pl.pallas_call(ladder_kernel, out_shape=jax.ShapeDtypeStruct((rows, n_ij)...]
where the time goes in v3:
time: 22.8 us; the launch traced here: 22.7 us
  Pallas kernels  21.2 us (93%)
  local copies, waits for them, and re-layouts  1.47 us (6%)
    pallas_call x1, Pallas kernels, in_place(): pl.pallas_call(ladder_kernel, out_shape=jax.ShapeDtypeStruct((rows, n_ij)...  21.2 us
    unnamed x1, local copies, waits for them, and re-layouts  1.47 us

profile of v3, /device:TPU:0, one launch (start us, length us, event | category | flops | bytes accessed | tf_op | source)
XLA Modules:
  0.0 22.7 jit_solution(9758120214580862457)
XLA Ops:
  0.0 21.2 %ladder.1 = bf16[16,2048]{1,0:T(8,128)(2,1)} custom-call(bf16[512,2048]{1,0:T(8,128)(2,1)} %amp_hbm.1, bf16[2048,128]{1,0:T(8,128)(2,1)} %int_hbm.1, f32[400]{0:T(512)} %occ_hbm.1, f32[1600]{0:T(1024)} %virt_hbm.1, s32[1600]{0:T(1024)} %irrep_hbm.1, s32[2,512]{1,0:T(2,128)} %bitcast.4, s32[2,256]{1,0:T(2,128)} %bitcast.5, s32[2,2048]{1,0:T(2,128)} %bitcast.3), custom_call_target="tpu_custom_call" | custom-call | tf_op jit(solution)/shard_map/ladder/pallas_call | solution.py:286
  21.2 1.5 %copy.10 = bf16[16,2048]{1,0:T(8,128)(2,1)} copy(bf16[16,2048]{1,0:T(8,128)(2,1)} %ladder.1) | data formatting | bytes 131072

commit v4 on v3

--- a/solution.py
+++ b/solution.py
@@ -8,7 +8,7 @@
 MESH = pl.DeviceIdType.MESH
 DEPTH = 256
 LAG = 2
-Y_FIRST = ((0, 2), (0, 1, 2))
+Y_FIRST = ((0, 1), (0, 2, 3))
 
 
 def three_parts(values):

time: 22.8 us -> 22.4 us (0.982)
  Pallas kernels: 21.2 us -> 20.8 us
    pallas_call x1, Pallas kernels: 21.2 us -> 20.8 us  [in_place(): pl.pallas_call(ladder_kernel, out_shape=jax.ShapeDtypeStruct((rows, n_ij)...]
where the time goes in v4:
time: 22.4 us; the launch traced here: 22.2 us
  Pallas kernels  20.8 us (93%)
  local copies, waits for them, and re-layouts  1.47 us (7%)
    pallas_call x1, Pallas kernels, in_place(): pl.pallas_call(ladder_kernel, out_shape=jax.ShapeDtypeStruct((rows, n_ij)...  20.8 us
    unnamed x1, local copies, waits for them, and re-layouts  1.47 us

profile of v4, /device:TPU:0, one launch (start us, length us, event | category | flops | bytes accessed | tf_op | source)
XLA Modules:
  0.0 22.2 jit_solution(9893149722819898073)
XLA Ops:
  0.0 20.8 %ladder.1 = bf16[16,2048]{1,0:T(8,128)(2,1)} custom-call(bf16[512,2048]{1,0:T(8,128)(2,1)} %amp_hbm.1, bf16[2048,128]{1,0:T(8,128)(2,1)} %int_hbm.1, f32[400]{0:T(512)} %occ_hbm.1, f32[1600]{0:T(1024)} %virt_hbm.1, s32[1600]{0:T(1024)} %irrep_hbm.1, s32[2,512]{1,0:T(2,128)} %bitcast.4, s32[2,256]{1,0:T(2,128)} %bitcast.5, s32[2,2048]{1,0:T(2,128)} %bitcast.3), custom_call_target="tpu_custom_call" | custom-call | tf_op jit(solution)/shard_map/ladder/pallas_call | solution.py:286
  20.8 1.5 %copy.10 = bf16[16,2048]{1,0:T(8,128)(2,1)} copy(bf16[16,2048]{1,0:T(8,128)(2,1)} %ladder.1) | data formatting | bytes 131072
